TPU v7x, 32 devices: a whole 2x2x4 slice. The times are simulated.
32 devices in a mesh: walk: 4 (over x, core), chol: 8 (over z, y).
Axes of the slice: x: 2, y: 2, z: 4, core: 2. Of those that a mesh axis runs over, the one named last changes fastest.
Arguments:
- walkers: bfloat16 [8, 8, 1024, 256], P('walk', 'chol'), may hold values from -1 to 2
- counts: int32 [8, 8], P('walk', 'chol'), may hold values from 0 to 3, as said below
- slot_copy: int32 [8, 8], P('walk', 'chol'), may hold values from 0 to 7, as said below
- factors: bfloat16 [8, 256, 1024], P('chol'), may hold values from -1.5 to 1.5
Outputs:
- combed: bfloat16 [8, 8, 1024, 256], P('walk', 'chol')
- gradient: float32 [8, 8, 1024, 256], P('walk', 'chol')
Inputs may be any that keep to these rules, and one draw needn't show every extreme that they name: In each population (column) the counts sum to 8. `slot_copy`: each column is a permutation of the copy numbers 0 to 7.
All inputs are finite; a program needn't handle non-finite values.
Results may differ from a plain program's by a relative error of at most 0.0068.
Values may be sent and summed in bfloat16 or wider, within the bound.
A program may use at most 64 MiB of HBM per device.

v0:
```python
import jax
import jax.numpy as jnp
from jax import lax
from jax.sharding import PartitionSpec as P

NEL = 256
NEWTON = 8


def shard_term(factor_block, green_block):
    rotated = jnp.einsum(
        "lrm,wmq->wlrq", factor_block, green_block, preferred_element_type=jnp.float32
    ).astype(jnp.bfloat16)
    shard_grad = -jnp.einsum(
        "lam,wlia->wmi", factor_block, rotated, preferred_element_type=jnp.float32
    )
    return lax.optimization_barrier(shard_grad.astype(jnp.bfloat16)).astype(jnp.float32)


def body(walkers, counts, slot_copy, factors):
    pop_counts = lax.all_gather(counts, "walk", axis=0, tiled=True)
    inclusive = jnp.cumsum(pop_counts[:, 0])
    wanted = slot_copy[:, 0]
    source = jnp.sum((inclusive[None, :] <= wanted[:, None]).astype(jnp.int32), axis=1)
    arrived = lax.all_gather(walkers, "walk", axis=0, tiled=True)
    height = arrived.shape[0]
    inside = (source >= 0) & (source < height)
    chosen = jnp.take(arrived, jnp.clip(source, 0, height - 1), axis=0)
    combed = jnp.where(inside[:, None, None, None], chosen, jnp.zeros_like(walkers))
    squares = combed[:, 0]
    intersection = squares[:, :NEL, :].astype(jnp.float32)
    identity = jnp.eye(NEL, dtype=jnp.float32)
    inverse = jnp.broadcast_to(identity, intersection.shape)
    for newton_step in range(NEWTON):
        product = jnp.einsum("wij,wjk->wik", intersection, inverse, precision=lax.Precision.HIGHEST)
        inverse = jnp.einsum(
            "wij,wjk->wik", inverse, 2.0 * identity - product, precision=lax.Precision.HIGHEST
        )
    green_block = jnp.einsum(
        "wmj,wji->wmi", squares, inverse.astype(jnp.bfloat16), preferred_element_type=jnp.float32
    ).astype(jnp.bfloat16)
    zero_grad = jnp.zeros(green_block.shape, jnp.float32)
    running = zero_grad
    shards = lax.all_gather(factors, "chol", axis=0, tiled=True).reshape((-1,) + factors.shape)

    def one_shard(partial_value, factor_block):
        return (partial_value + shard_term(factor_block, green_block), None)

    running, unused = lax.scan(one_shard, running, shards)
    return (combed, running[:, None])


def solution(mesh):
    in_specs = (
        P("walk", "chol", None, None),
        P("walk", "chol"),
        P("walk", "chol"),
        P("chol", None, None),
    )
    out_specs = (P("walk", "chol", None, None), P("walk", "chol", None, None))
    return jax.shard_map(body, mesh=mesh, in_specs=in_specs, out_specs=out_specs, check_vma=False)
```

profile of v0, /device:TPU:0, one launch (start us, length us, event | category | flops | bytes accessed | tf_op | source)
XLA Modules:
  0.0 155.3 jit_solution(9308151468120643752)
XLA Ops:
  7.2 0.7 all-gather.3.cloned.1.call-update
  7.9 0.7 all-gather.5.cloned.1.call-update
  8.7 1.2 dynamic-slice
  10.6 0.8 bitcast_dynamic-update-slice_fusion
  11.3 6.3 %all-reduce = s32[8]{0:T(128)S(1)} all-reduce(s32[8]{0:T(128)S(1)} %bitcast_dynamic-update-slice_fusion), channel_id=1, replica_groups=mesh['walk'=4,'chol'=8] {'walk'}, use_global_device_ids=true, to_apply=%add | all-reduce | flops 8 | bytes 64
  17.8 0.8 fusion.23
  18.7 0.7 fusion.14
  19.5 27.3 %all-gather.3.cloned.1.call-done = bf16[8,1,1024,256]{3,2,1,0:T(8,128)(2,1)} async-done(((bf16[2,1,1024,256]{3,2,1,0:T(8,128)(2,1)}), bf16[8,1,1024,256]{3,2,1,0:T(8,128)(2,1)}) %all-gather.3.cloned.1.call-update) | async-done | bytes 4194320 | tf_op jit(solution)/shard_map/all_gather | solution.py:25
  46.8 2.8 %gather_fusion = bf16[2,1024,256]{2,1,0:T(8,128)(2,1)S(1)} fusion(bf16[8,1024,256]{2,1,0:T(8,128)(2,1)} %bitcast.77, s32[1024]{0:T(1024)S(1)} %pad_clamp_fusion), kind=kCustom, calls=%fused_computation | custom fusion | bytes 2097160 | tf_op jit(solution)/shard_map/jit(_take)/gather | solution.py:28
  49.8 0.8 copy-done
  53.1 0.7 fusion.26
  59.4 1.2 fusion.9
  60.5 1.4 convolution_convert_fusion.1
  61.9 60.4 %all-gather.5.cloned.1.call-done = bf16[8,256,1024]{2,1,0:T(8,128)(2,1)} async-done(((bf16[1,256,1024]{2,1,0:T(8,128)(2,1)}), bf16[8,256,1024]{2,1,0:T(8,128)(2,1)}) %all-gather.5.cloned.1.call-update) | async-done | bytes 4194320 | tf_op jit(solution)/shard_map/all_gather | solution.py:44
  122.3 24.3 %while.11 = (s32[]{:T(128)}, f32[2,1024,256]{1,2,0:T(8,128)S(1)}, bf16[8,1,256,1024]{3,2,1,0:T(8,128)(2,1)}, bf16[2,1024,256]{2,1,0:T(8,128)(2,1)}, s32[]{:T(128)}, /*index=5*/s32[]{:T(128)}) while((s32[]{:T(128)}, f32[2,1024,256]{1,2,0:T(8,128)S(1)}, bf16[8,1,256,1024]{3,2,1,0:T(8,128)(2,1)}, bf16[2,1024,256]{2,1,0:T(8,128)(2,1)}, ...), condition=%wide.region_3.4_spmd.clone, body=%wide.region_2.3_spmd.clone.sunk | while | flops 539623424 | bytes 8389719 | solution.py:49
  122.3 2.3 %fusion.63 = bf16[2,1024,256]{1,2,0:T(8,128)(2,1)S(1)} fusion(bf16[2,1024,256]{2,1,0:T(8,128)(2,1)} %get-tuple-element.102, bf16[8,1,256,1024]{3,2,1,0:T(8,128)(2,1)} %get-tuple-element.101, s32[]{:T(128)S(6)} %copy.16), kind=kOutput, calls=%fused_computation.3.clone.1 | convolution fusion | flops 538050560 | bytes 3146752 | tf_op jit(solution)/shard_map/while/body/eval_jaxpr/lam,wlia->wmi/dot_general | solution.py:14
  124.6 0.7 select_add_fusion.2
  125.3 2.4 %fusion.63 = bf16[2,1024,256]{1,2,0:T(8,128)(2,1)S(1)} fusion(bf16[2,1024,256]{2,1,0:T(8,128)(2,1)} %get-tuple-element.102, bf16[8,1,256,1024]{3,2,1,0:T(8,128)(2,1)} %get-tuple-element.101, s32[]{:T(128)S(6)} %copy.16), kind=kOutput, calls=%fused_computation.3.clone.1 | convolution fusion | flops 538050560 | bytes 3146752 | tf_op jit(solution)/shard_map/while/body/eval_jaxpr/lam,wlia->wmi/dot_general | solution.py:14
  127.7 0.7 select_add_fusion.2
  128.4 2.3 %fusion.63 = bf16[2,1024,256]{1,2,0:T(8,128)(2,1)S(1)} fusion(bf16[2,1024,256]{2,1,0:T(8,128)(2,1)} %get-tuple-element.102, bf16[8,1,256,1024]{3,2,1,0:T(8,128)(2,1)} %get-tuple-element.101, s32[]{:T(128)S(6)} %copy.16), kind=kOutput, calls=%fused_computation.3.clone.1 | convolution fusion | flops 538050560 | bytes 3146752 | tf_op jit(solution)/shard_map/while/body/eval_jaxpr/lam,wlia->wmi/dot_general | solution.py:14
  130.7 0.7 select_add_fusion.2
  131.5 2.4 %fusion.63 = bf16[2,1024,256]{1,2,0:T(8,128)(2,1)S(1)} fusion(bf16[2,1024,256]{2,1,0:T(8,128)(2,1)} %get-tuple-element.102, bf16[8,1,256,1024]{3,2,1,0:T(8,128)(2,1)} %get-tuple-element.101, s32[]{:T(128)S(6)} %copy.16), kind=kOutput, calls=%fused_computation.3.clone.1 | convolution fusion | flops 538050560 | bytes 3146752 | tf_op jit(solution)/shard_map/while/body/eval_jaxpr/lam,wlia->wmi/dot_general | solution.py:14
  133.8 0.7 select_add_fusion.2
  134.5 2.3 %fusion.63 = bf16[2,1024,256]{1,2,0:T(8,128)(2,1)S(1)} fusion(bf16[2,1024,256]{2,1,0:T(8,128)(2,1)} %get-tuple-element.102, bf16[8,1,256,1024]{3,2,1,0:T(8,128)(2,1)} %get-tuple-element.101, s32[]{:T(128)S(6)} %copy.16), kind=kOutput, calls=%fused_computation.3.clone.1 | convolution fusion | flops 538050560 | bytes 3146752 | tf_op jit(solution)/shard_map/while/body/eval_jaxpr/lam,wlia->wmi/dot_general | solution.py:14
  136.8 0.7 select_add_fusion.2
  137.5 2.3 %fusion.63 = bf16[2,1024,256]{1,2,0:T(8,128)(2,1)S(1)} fusion(bf16[2,1024,256]{2,1,0:T(8,128)(2,1)} %get-tuple-element.102, bf16[8,1,256,1024]{3,2,1,0:T(8,128)(2,1)} %get-tuple-element.101, s32[]{:T(128)S(6)} %copy.16), kind=kOutput, calls=%fused_computation.3.clone.1 | convolution fusion | flops 538050560 | bytes 3146752 | tf_op jit(solution)/shard_map/while/body/eval_jaxpr/lam,wlia->wmi/dot_general | solution.py:14
  139.9 0.7 select_add_fusion.2
  140.6 2.3 %fusion.63 = bf16[2,1024,256]{1,2,0:T(8,128)(2,1)S(1)} fusion(bf16[2,1024,256]{2,1,0:T(8,128)(2,1)} %get-tuple-element.102, bf16[8,1,256,1024]{3,2,1,0:T(8,128)(2,1)} %get-tuple-element.101, s32[]{:T(128)S(6)} %copy.16), kind=kOutput, calls=%fused_computation.3.clone.1 | convolution fusion | flops 538050560 | bytes 3146752 | tf_op jit(solution)/shard_map/while/body/eval_jaxpr/lam,wlia->wmi/dot_general | solution.py:14
  142.9 0.7 select_add_fusion.2
  143.6 2.3 %fusion.63 = bf16[2,1024,256]{1,2,0:T(8,128)(2,1)S(1)} fusion(bf16[2,1024,256]{2,1,0:T(8,128)(2,1)} %get-tuple-element.102, bf16[8,1,256,1024]{3,2,1,0:T(8,128)(2,1)} %get-tuple-element.101, s32[]{:T(128)S(6)} %copy.16), kind=kOutput, calls=%fused_computation.3.clone.1 | convolution fusion | flops 538050560 | bytes 3146752 | tf_op jit(solution)/shard_map/while/body/eval_jaxpr/lam,wlia->wmi/dot_general | solution.py:14
  145.9 0.7 select_add_fusion.2
  146.6 1.8 %copy.11 = f32[2,1024,256]{2,1,0:T(8,128)} copy(f32[2,1024,256]{1,2,0:T(8,128)S(1)} %get-tuple-element.24) | data formatting | bytes 4194304 | tf_op jit(solution)/shard_map/while | solution.py:49
  (26 shorter events, 8.6 us)
Async XLA Ops:
  7.2 39.6 %all-gather.3.cloned.1.call-start = ((), (), s32[]{:S(2)}) async-start(), calls=%async_computation | async-start | bytes 5242880 | tf_op jit(solution)/shard_map/all_gather | solution.py:25
  7.9 114.4 %all-gather.5.cloned.1.call-start = ((), (), s32[]{:S(2)}) async-start(), calls=%async_computation.1 | async-start | bytes 4718592 | tf_op jit(solution)/shard_map/all_gather | solution.py:44
  49.6 1.0 copy-start
Sparse Core Ops, SparseCore 0:
  9.6 37.1 all-gather.2
  48.9 73.3 all-gather.4
where the time goes:
time: 156 us; the launch traced here: 155 us
  waiting for transfers between devices  89.1 us (57%)
  matrix products  28.7 us (18%)
  between operations  14.9 us (10%)
  other arithmetic  8.61 us (6%)
  local copies, waits for them, and re-layouts  7.37 us (5%)
  blocking collectives  6.35 us (4%)
    all_gather x1, waiting for transfers between devices, body(): lax.all_gather(factors, 'chol', axis=0, tiled=True)  60.4 us
    all_gather x1, waiting for transfers between devices, body(): arrived = lax.all_gather(walkers, 'walk', axis=0, tiled=True)  27.3 us
    dot_general x8, matrix products, shard_term(): jnp.einsum('lam,wlia->wmi', factor_block, rotated, preferred_element_type...  18.6 us
    unnamed x1, blocking collectives  6.35 us
    add x8, other arithmetic, one_shard(): return (partial_value + shard_term(factor_block, green_block), None)  5.48 us
    dot_general x8, matrix products, body(): jnp.einsum('wij,wjk->wik', inverse, 2.0 * identity - product, precision=l...  5.22 us
    dot_general x8, matrix products, body(): jnp.einsum('wij,wjk->wik', intersection, inverse, precision=lax.Precision...  3.51 us
  transfers between devices with their start and end apart: 2, of which 2 were waited for; matrix products, arithmetic and copies ran while one was open for 12% of the time, Pallas kernels for 0%

commit v1 on v0

v1 whole, which is shorter than its diff:
```python
import functools

import jax
import jax.numpy as jnp
from jax import lax
from jax.experimental import pallas as pl
from jax.experimental.pallas import tpu as pltpu
from jax.sharding import PartitionSpec as P

NEWTON = 8
MESH = pl.DeviceIdType.MESH
F32 = jnp.float32
BF16 = jnp.bfloat16


def kernel(nw, nc, cnt_ref, slot_ref, f_ref, w_ref, comb_ref, grad_ref, *scratch):
    per, rows, nel = w_ref.shape
    nch = rows // nel
    pop = nw * per
    arr = scratch[:nch]
    (full, cbuf, call, csm, ex, inv, green, racc, rt,
     csend, crecv, csem, wsem, rsem, fsem) = scratch[nch:]
    half = nc // 2
    chips = nw // 2
    part = rows // 4

    me = lax.axis_index("walk")
    col = lax.axis_index("chol")
    core = me % 2
    chip = me // 2
    sib = chip * 2 + (1 - core)
    odd = col % 2
    pos = (1 - odd) * (col // 2) + odd * (nc - 1 - col // 2)

    def at_pos(p):
        p = (p + 2 * nc) % nc
        hi = p // half
        return (1 - hi) * (2 * p) + hi * (2 * (nc - 1 - p) + 1)

    right, left = at_pos(pos + 1), at_pos(pos - 1)

    barrier = pltpu.get_barrier_semaphore()
    for k in range(1, nw):
        pl.semaphore_signal(barrier, inc=1, device_id=((me + k) % nw, col), device_id_type=MESH)
    for nb in (left, right):
        pl.semaphore_signal(barrier, inc=1, device_id=(me, nb), device_id_type=MESH)
    lane = lax.broadcasted_iota(jnp.int32, cbuf.shape, 1)
    packed = jnp.zeros(cbuf.shape, jnp.int32)
    for i in range(per):
        packed = jnp.where(lane == i, cnt_ref[i, 0], packed)
    cbuf[...] = packed
    pl.semaphore_wait(barrier, nw + 1)

    sends = []

    def remote(src, dst, ssem, rsem_, dev):
        return pltpu.make_async_remote_copy(
            src_ref=src, dst_ref=dst, send_sem=ssem, recv_sem=rsem_,
            device_id=dev, device_id_type=MESH)

    def go(copy):
        copy.start()
        sends.append(copy)

    def chunk(ch):
        return pl.ds(ch * nel, nel)

    def wx(ch, d):
        to = ((chip + d) % chips) * 2 + core
        return remote(w_ref.at[:, chunk(ch)], arr[ch].at[pl.ds(me * per, per)],
                      wsem.at[0, ch, d], wsem.at[1, ch, d], (to, col))

    def wx_in(ch, d):
        origin = ((chip - d + chips) % chips) * 2 + core
        return arr[ch].at[pl.ds(origin * per, per)]

    def ws(ch):
        return remote(w_ref.at[:, chunk(ch)], arr[ch].at[pl.ds(me * per, per)],
                      wsem.at[0, ch, 0], wsem.at[1, ch, 0], (sib, col))

    def wf(ch, d):
        block = wx_in(ch, d)
        return remote(block, block, wsem.at[2, ch, d], wsem.at[3, ch, d], (sib, col))

    def own(ch):
        return pltpu.make_async_copy(
            w_ref.at[:, chunk(ch)], arr[ch].at[pl.ds(me * per, per)], wsem.at[2, ch, 0])

    def landed(ref, sem):
        remote(ref, ref, sem, sem, (sib, col)).wait_recv()

    def walkers_in(ch):
        for d in range(1, chips):
            landed(wx_in(ch, d), wsem.at[1, ch, d])
            go(wf(ch, d))
        if ch + 2 < nch:
            for d in range(1, chips):
                go(wx(ch + 2, d))

    def walkers_all(ch):
        own(ch).wait()
        landed(arr[ch].at[pl.ds(sib * per, per)], wsem.at[1, ch, 0])
        for d in range(1, chips):
            origin = ((chip - d + chips) % chips) * 2 + (1 - core)
            landed(arr[ch].at[pl.ds(origin * per, per)], wsem.at[3, ch, d])

    for k in range(1, nw):
        go(remote(cbuf, call.at[me], csend.at[k], crecv.at[k], ((me + k) % nw, col)))
    for ch in range(min(2, nch)):
        for d in range(1, chips):
            go(wx(ch, d))
    for ch in range(nch):
        own(ch).start()
        go(ws(ch))

    for m in range(0, rows, nel):
        full[col, m:m + nel, :] = f_ref[:, m:m + nel].T

    def piece(origin, c, j):
        return full.at[origin, pl.ds((c * 2 + j) * part, part)]

    def ring(s, j, way):
        origin = at_pos(pos - (s - 1) if way == 0 else pos + (s - 1))
        block = piece(origin, core, j)
        return remote(block, block, rsem.at[0, way, s - 1, j], rsem.at[1, way, s - 1, j],
                      (me, right if way == 0 else left))

    def ways(s, j):
        return (0, 1) if s < half else (j,)

    def source_of(s, way):
        return at_pos(pos - s if way == 0 else pos + s)

    def factor_in(s, j):
        for way in ways(s, j):
            block = piece(source_of(s, way), core, j)
            landed(block, rsem.at[1, way, s - 1, j])
            if s < half and way in ways(s + 1, j):
                go(ring(s + 1, j, way))
            go(remote(block, block, fsem.at[0, way, s - 1, j], fsem.at[1, way, s - 1, j],
                      (sib, col)))

    def factor_all():
        for s in range(1, half + 1):
            for j in range(2):
                for way in ways(s, j):
                    landed(piece(source_of(s, way), 1 - core, j), fsem.at[1, way, s - 1, j])

    for j in range(2):
        for way in ways(1, j):
            go(ring(1, j, way))
    events = [(s, j) for s in range(1, half + 1) for j in range(2)]

    def pump(count):
        for _ in range(min(count, len(events))):
            factor_in(*events.pop(0))

    pump(2)
    walkers_in(0)

    call[me] = packed
    for k in range(1, nw):
        landed(call.at[(me - k + nw) % nw], crecv.at[k])
    to_smem = pltpu.make_async_copy(call, csm, csem.at[0])
    to_smem.start()
    to_smem.wait()
    wanted = [slot_ref[i, 0] for i in range(per)]
    chosen = [jnp.int32(0) for _ in range(per)]
    total = jnp.int32(0)
    for i in range(pop):
        total = total + csm[i // per, 0, i % per]
        for w in range(per):
            chosen[w] = chosen[w] + (total <= wanted[w]).astype(jnp.int32)
    chosen = [jnp.minimum(c, pop - 1) for c in chosen]

    def select(ch, w):
        block = arr[ch][chosen[w]]
        comb_ref[w, ch * nel:(ch + 1) * nel, :] = block
        return block.T

    eye = (lax.broadcasted_iota(jnp.int32, (nel, nel), 0)
           == lax.broadcasted_iota(jnp.int32, (nel, nel), 1)).astype(F32)
    walkers_all(0)
    tops = [select(0, w) for w in range(per)]
    for w in range(per):
        ex[w, :nel, :] = eye - tops[w].astype(F32)
        ex[w, nel:, :] = eye

    def newton(steps):
        def step(_, carry):
            for w in range(per):
                both = ex[w]
                prod = jnp.dot(both, both[:nel], precision=lax.Precision.HIGHEST,
                               preferred_element_type=F32)
                ex[w, :nel, :] = prod[:nel]
                ex[w, nel:, :] = both[nel:] + prod[nel:]
            return carry
        lax.fori_loop(0, steps, step, 0)

    def make_green(ch, flipped):
        for w in range(per):
            green[w * nel:(w + 1) * nel, ch * nel:(ch + 1) * nel] = jnp.dot(
                inv[w], flipped[w], preferred_element_type=F32).astype(BF16)

    def combine(ch):
        walkers_all(ch)
        make_green(ch, [select(ch, w) for w in range(per)])

    third = (NEWTON + 2) // 3
    newton(third)
    pump(1)
    newton(third)
    pump(1)
    walkers_in(1)
    newton(NEWTON - 2 * third)
    for w in range(per):
        inv[w] = ex[w, nel:, :].astype(BF16)
    make_green(0, tops)
    combine(1)
    pump(2)
    for ch in range(2, nch - 1):
        walkers_in(ch)
        combine(ch)
    pump(len(events))
    factor_all()
    lead = rows - nel

    def rotate_lead(l, carry):
        racc[l] = jnp.dot(green[:, :lead], full[l, :lead, :], preferred_element_type=F32)
        return carry

    lax.fori_loop(0, nc, rotate_lead, 0)
    walkers_in(nch - 1)
    combine(nch - 1)

    def rotate_last(l, carry):
        r = racc[l] + jnp.dot(green[:, lead:], full[l, lead:, :], preferred_element_type=F32)
        for w in range(per):
            rt[w, l] = r[w * nel:(w + 1) * nel].astype(BF16)
        return carry

    lax.fori_loop(0, nc, rotate_last, 0)

    def finish(b, carry):
        at = pl.ds(pl.multiple_of(b * nel, nel), nel)
        lhs = jnp.concatenate([full[l, at, :] for l in range(nc)], axis=1)
        for w in range(per):
            rhs = rt[w].reshape(nc * nel, nel)
            grad_ref[w, at, :] = -jnp.dot(lhs, rhs, preferred_element_type=F32)
        return carry

    lax.fori_loop(0, nch, finish, 0)
    for copy in sends:
        copy.wait_send()


def body(nw, nc, walkers, counts, slot_copy, factors):
    per, _, rows, nel = walkers.shape
    nch = rows // nel
    pop = nw * per
    vmem = pl.BlockSpec(memory_space=pltpu.VMEM)
    smem = pl.BlockSpec(memory_space=pltpu.SMEM)
    dma = pltpu.SemaphoreType.DMA
    half = nc // 2
    combed, grad = pl.pallas_call(
        functools.partial(kernel, nw, nc),
        out_shape=(
            jax.ShapeDtypeStruct((per, rows, nel), BF16),
            jax.ShapeDtypeStruct((per, rows, nel), F32),
        ),
        in_specs=[smem, smem, vmem, pl.BlockSpec(memory_space=pl.ANY)],
        out_specs=(vmem, vmem),
        scratch_shapes=[pltpu.VMEM((pop, nel, nel), BF16)] * nch + [
            pltpu.VMEM((nc, rows, nel), BF16),
            pltpu.VMEM((8, 128), jnp.int32),
            pltpu.VMEM((nw, 8, 128), jnp.int32),
            pltpu.SMEM((nw, 8, 128), jnp.int32),
            pltpu.VMEM((per, 2 * nel, nel), F32),
            pltpu.VMEM((per, nel, nel), BF16),
            pltpu.VMEM((per * nel, rows), BF16),
            pltpu.VMEM((nc, per * nel, nel), F32),
            pltpu.VMEM((per, nc, nel, nel), BF16),
            dma((nw,)),
            dma((nw,)),
            dma((1,)),
            dma((4, nch, nw // 2)),
            dma((2, 2, half, 2)),
            dma((2, 2, half, 2)),
        ],
        compiler_params=pltpu.CompilerParams(
            collective_id=0, has_side_effects=True, vmem_limit_bytes=56 << 20),
    )(counts, slot_copy, factors[0], walkers[:, 0])
    return combed[:, None], grad[:, None]


def solution(mesh):
    nw, nc = mesh.shape["walk"], mesh.shape["chol"]
    wide = P("walk", "chol", None, None)
    flat = P("walk", "chol")
    return jax.shard_map(
        functools.partial(body, nw, nc), mesh=mesh,
        in_specs=(wide, flat, flat, P("chol", None, None)),
        out_specs=(wide, wide), check_vma=False)
```

time: 156 us -> 51.7 us (0.33)
  waiting for transfers between devices: 89.1 us -> 0 us
  Pallas kernels: 0 us -> 44.5 us
  matrix products: 28.7 us -> 0 us
  between operations: 14.9 us -> 0.65 us
  other arithmetic: 8.61 us -> 0 us
  blocking collectives: 6.35 us -> 0 us
    all_gather x2 -> x0, waiting for transfers between devices: 87.7 us -> none  [the longest x1 60.4 us: body(): lax.all_gather(factors, 'chol', axis=0, tiled=True)]
    pallas_call x0 -> x1, Pallas kernels: none -> 44.5 us  [body(): pl.pallas_call(functools.partial(kernel, nw, nc), out_shape=(jax.ShapeDty...]
    dot_general x25 -> x0, matrix products: 28.7 us -> none  [the longest x8 18.6 us: shard_term(): jnp.einsum('lam,wlia->wmi', factor_block, rotated, preferred_element_type...]
    unnamed x1 -> x0, blocking collectives: 6.35 us -> none
    add x8 -> x0, other arithmetic: 5.48 us -> none  [one_shard(): return (partial_value + shard_term(factor_block, green_block), None)]
    unnamed x5 -> x6, local copies, waits for them, and re-layouts: 2.76 us -> 6.33 us
    gather x1 -> x0, local copies, waits for them, and re-layouts: 2.8 us -> none  [body(): chosen = jnp.take(arrived, jnp.clip(source, 0, height - 1), axis=0)]
    while x1 -> x0, local copies, waits for them, and re-layouts: 1.81 us -> none  [body(): running, unused = lax.scan(one_shard, running, shards)]
  transfers between devices with their start and end apart: 2 -> 0, of which waited for: 2 -> 0; matrix products, arithmetic and copies ran while one was open for 12% -> 0% of each run, Pallas kernels for 0% -> 0%
where the time goes in v1:
time: 51.7 us; the launch traced here: 51.5 us
  Pallas kernels  44.5 us (86%)
  local copies, waits for them, and re-layouts  6.33 us (12%)
  between operations  0.65 us (1%)
    pallas_call x1, Pallas kernels, body(): pl.pallas_call(functools.partial(kernel, nw, nc), out_shape=(jax.ShapeDty...  44.5 us
    unnamed x6, local copies, waits for them, and re-layouts  6.33 us

profile of v1, /device:TPU:0, one launch (start us, length us, event | category | flops | bytes accessed | tf_op | source)
XLA Modules:
  0.0 51.5 jit_solution(775909052680926238)
XLA Ops:
  0.6 1.3 %copy.6.cnt_ref = s32[2,1]{1,0:T(2,128)} copy(s32[2,1]{0,1:T(1,128)} %param.5) | data formatting | bytes 16 | tf_op args[1]
  1.9 1.3 %copy.7.slot_ref = s32[2,1]{1,0:T(2,128)} copy(s32[2,1]{0,1:T(1,128)} %param.6) | data formatting | bytes 16 | tf_op args[2]
  3.2 44.5 %shard_map.59 = (bf16[2,1024,256]{2,1,0:T(8,128)(2,1)}, f32[2,1024,256]{2,1,0:T(8,128)}) custom-call(s32[2,1]{1,0:T(2,128)} %copy.6.cnt_ref, s32[2,1]{1,0:T(2,128)} %copy.7.slot_ref, bf16[256,1024]{1,0:T(8,128)(2,1)} %bitcast.11, bf16[2,1024,256]{2,1,0:T(8,128)(2,1)} %bitcast.9), custom_call_target="tpu_custom_call" | custom-call | tf_op jit(solution)/shard_map/pallas_call | solution.py:265
  47.7 0.0 copy-start
  47.8 2.4 %copy.12 = bf16[2,1,1024,256]{3,2,1,0:T(8,128)(2,1)} copy(bf16[2,1,1024,256]{3,2,1,0:T(8,128)(2,1)} %bitcast.10) | data formatting | bytes 2097152
  50.2 0.0 copy-done
  50.2 1.3 %copy.13 = f32[2,1,1024,256]{3,2,1,0:T(8,128)} copy(f32[2,1,1024,256]{3,2,1,0:T(8,128)S(1)} %bitcast.8) | data formatting | bytes 4194304
Async XLA Ops:
  47.7 2.4 %copy-start = (f32[2,1024,256]{2,1,0:T(8,128)S(1)}, f32[2,1024,256]{2,1,0:T(8,128)}, u32[]{:S(2)}) copy-start(f32[2,1024,256]{2,1,0:T(8,128)} %get-tuple-element.5) | copy-start | bytes 6291460

commit v2 on v1

--- a/solution.py
+++ b/solution.py
@@ -13,13 +13,13 @@
 BF16 = jnp.bfloat16
 
 
-def kernel(nw, nc, cnt_ref, slot_ref, f_ref, w_ref, comb_ref, grad_ref, *scratch):
+def kernel(nw, nc, cnt_ref, slot_ref, f_ref, w_ref, comb_out, grad_out, *scratch):
     per, rows, nel = w_ref.shape
     nch = rows // nel
     pop = nw * per
     arr = scratch[:nch]
     (full, cbuf, call, csm, ex, inv, green, racc, rt,
-     csend, crecv, csem, wsem, rsem, fsem) = scratch[nch:]
+     comb_ref, grad_ref, osem, csend, crecv, csem, wsem, rsem, fsem) = scratch[nch:]
     half = nc // 2
     chips = nw // 2
     part = rows // 4
@@ -47,11 +47,11 @@
     lane = lax.broadcasted_iota(jnp.int32, cbuf.shape, 1)
     packed = jnp.zeros(cbuf.shape, jnp.int32)
     for i in range(per):
-        packed = jnp.where(lane == i, cnt_ref[i, 0], packed)
+        packed = jnp.where(lane == i, cnt_ref[0, i], packed)
     cbuf[...] = packed
     pl.semaphore_wait(barrier, nw + 1)
 
-    sends = []
+    sends, outs = [], []
 
     def remote(src, dst, ssem, rsem_, dev):
         return pltpu.make_async_remote_copy(
@@ -106,9 +106,8 @@
 
     for k in range(1, nw):
         go(remote(cbuf, call.at[me], csend.at[k], crecv.at[k], ((me + k) % nw, col)))
-    for ch in range(min(2, nch)):
-        for d in range(1, chips):
-            go(wx(ch, d))
+    for d in range(1, chips):
+        go(wx(0, d))
     for ch in range(nch):
         own(ch).start()
         go(ws(ch))
@@ -155,7 +154,10 @@
         for _ in range(min(count, len(events))):
             factor_in(*events.pop(0))
 
-    pump(2)
+    pump(1)
+    for d in range(1, chips):
+        go(wx(1, d))
+    pump(1)
     walkers_in(0)
 
     call[me] = packed
@@ -164,7 +166,7 @@
     to_smem = pltpu.make_async_copy(call, csm, csem.at[0])
     to_smem.start()
     to_smem.wait()
-    wanted = [slot_ref[i, 0] for i in range(per)]
+    wanted = [slot_ref[0, i] for i in range(per)]
     chosen = [jnp.int32(0) for _ in range(per)]
     total = jnp.int32(0)
     for i in range(pop):
@@ -176,6 +178,10 @@
     def select(ch, w):
         block = arr[ch][chosen[w]]
         comb_ref[w, ch * nel:(ch + 1) * nel, :] = block
+        out = pltpu.make_async_copy(comb_ref.at[w, chunk(ch)], comb_out.at[w, chunk(ch)],
+                                    osem.at[w, ch])
+        out.start()
+        outs.append(out)
         return block.T
 
     eye = (lax.broadcasted_iota(jnp.int32, (nel, nel), 0)
@@ -190,8 +196,11 @@
         def step(_, carry):
             for w in range(per):
                 both = ex[w]
-                prod = jnp.dot(both, both[:nel], precision=lax.Precision.HIGHEST,
-                               preferred_element_type=F32)
+                high = both.astype(BF16)
+                low = (both - high.astype(F32)).astype(BF16)
+                prod = (jnp.dot(high, high[:nel], preferred_element_type=F32)
+                        + (jnp.dot(high, low[:nel], preferred_element_type=F32)
+                           + jnp.dot(low, high[:nel], preferred_element_type=F32)))
                 ex[w, :nel, :] = prod[:nel]
                 ex[w, nel:, :] = both[nel:] + prod[nel:]
             return carry
@@ -241,15 +250,15 @@
 
     lax.fori_loop(0, nc, rotate_last, 0)
 
-    def finish(b, carry):
-        at = pl.ds(pl.multiple_of(b * nel, nel), nel)
-        lhs = jnp.concatenate([full[l, at, :] for l in range(nc)], axis=1)
-        for w in range(per):
-            rhs = rt[w].reshape(nc * nel, nel)
-            grad_ref[w, at, :] = -jnp.dot(lhs, rhs, preferred_element_type=F32)
-        return carry
-
-    lax.fori_loop(0, nch, finish, 0)
+    for w in range(per):
+        lhs = jnp.concatenate([full[l] for l in range(nc)], axis=1)
+        rhs = rt[w].reshape(nc * nel, nel)
+        grad_ref[w] = -jnp.dot(lhs, rhs, preferred_element_type=F32)
+        out = pltpu.make_async_copy(grad_ref.at[w], grad_out.at[w], osem.at[w, nch])
+        out.start()
+        outs.append(out)
+    for out in outs:
+        out.wait()
     for copy in sends:
         copy.wait_send()
 
@@ -269,7 +278,7 @@
             jax.ShapeDtypeStruct((per, rows, nel), F32),
         ),
         in_specs=[smem, smem, vmem, pl.BlockSpec(memory_space=pl.ANY)],
-        out_specs=(vmem, vmem),
+        out_specs=(pl.BlockSpec(memory_space=pl.ANY),) * 2,
         scratch_shapes=[pltpu.VMEM((pop, nel, nel), BF16)] * nch + [
             pltpu.VMEM((nc, rows, nel), BF16),
             pltpu.VMEM((8, 128), jnp.int32),
@@ -280,6 +289,9 @@
             pltpu.VMEM((per * nel, rows), BF16),
             pltpu.VMEM((nc, per * nel, nel), F32),
             pltpu.VMEM((per, nc, nel, nel), BF16),
+            pltpu.VMEM((per, rows, nel), BF16),
+            pltpu.VMEM((per, rows, nel), F32),
+            dma((per, nch + 1)),
             dma((nw,)),
             dma((nw,)),
             dma((1,)),
@@ -289,7 +301,7 @@
         ],
         compiler_params=pltpu.CompilerParams(
             collective_id=0, has_side_effects=True, vmem_limit_bytes=56 << 20),
-    )(counts, slot_copy, factors[0], walkers[:, 0])
+    )(counts.T, slot_copy.T, factors[0], walkers[:, 0])
     return combed[:, None], grad[:, None]
 
 

time: 51.7 us -> 46.7 us (0.903)
  local copies, waits for them, and re-layouts: 6.33 us -> 3.73 us
  Pallas kernels: 44.5 us -> 42.2 us
    unnamed x6 -> x4, local copies, waits for them, and re-layouts: 6.33 us -> 3.73 us
    pallas_call x1, Pallas kernels: 44.5 us -> 42.2 us  [body(): pl.pallas_call(functools.partial(kernel, nw, nc), out_shape=(jax.ShapeDty...]
where the time goes in v2:
time: 46.7 us; the launch traced here: 46.5 us
  Pallas kernels  42.2 us (90%)
  local copies, waits for them, and re-layouts  3.73 us (8%)
  between operations  0.65 us (1%)
    pallas_call x1, Pallas kernels, body(): pl.pallas_call(functools.partial(kernel, nw, nc), out_shape=(jax.ShapeDty...  42.2 us
    unnamed x4, local copies, waits for them, and re-layouts  3.73 us

profile of v2, /device:TPU:0, one launch (start us, length us, event | category | flops | bytes accessed | tf_op | source)
XLA Modules:
  0.0 46.5 jit_solution(11143896251556874054)
XLA Ops:
  0.6 42.2 %shard_map.59 = (bf16[2,1024,256]{2,1,0:T(8,128)(2,1)}, f32[2,1024,256]{2,1,0:T(8,128)}) custom-call(s32[1,2]{1,0:T(1,128)} %bitcast.14, s32[1,2]{1,0:T(1,128)} %bitcast.15, bf16[256,1024]{1,0:T(8,128)(2,1)} %bitcast.13, bf16[2,1024,256]{2,1,0:T(8,128)(2,1)} %bitcast.11), custom_call_target="tpu_custom_call" | custom-call | tf_op jit(solution)/shard_map/pallas_call | solution.py:274
  42.8 0.0 copy-start
  42.8 2.4 %copy.10 = bf16[2,1,1024,256]{3,2,1,0:T(8,128)(2,1)} copy(bf16[2,1,1024,256]{3,2,1,0:T(8,128)(2,1)} %bitcast.12) | data formatting | bytes 2097152
  45.2 0.0 copy-done
  45.2 1.3 %copy.11 = f32[2,1,1024,256]{3,2,1,0:T(8,128)} copy(f32[2,1,1024,256]{3,2,1,0:T(8,128)S(1)} %bitcast.10) | data formatting | bytes 4194304
Async XLA Ops:
  42.8 2.4 %copy-start = (f32[2,1024,256]{2,1,0:T(8,128)S(1)}, f32[2,1024,256]{2,1,0:T(8,128)}, u32[]{:S(2)}) copy-start(f32[2,1024,256]{2,1,0:T(8,128)} %get-tuple-element.5) | copy-start | bytes 6291460

commit v3 on v2

--- a/solution.py
+++ b/solution.py
@@ -19,7 +19,7 @@
     pop = nw * per
     arr = scratch[:nch]
     (full, cbuf, call, csm, ex, inv, green, racc, rt,
-     comb_ref, grad_ref, osem, csend, crecv, csem, wsem, rsem, fsem) = scratch[nch:]
+     comb_ref, grad_ref, osem, csend, crecv, csem, wsem, xsem, rsem, fsem) = scratch[nch:]
     half = nc // 2
     chips = nw // 2
     part = rows // 4
@@ -65,22 +65,24 @@
     def chunk(ch):
         return pl.ds(ch * nel, nel)
 
-    def wx(ch, d):
+    def wx(ch, d, h):
         to = ((chip + d) % chips) * 2 + core
-        return remote(w_ref.at[:, chunk(ch)], arr[ch].at[pl.ds(me * per, per)],
-                      wsem.at[0, ch, d], wsem.at[1, ch, d], (to, col))
-
-    def wx_in(ch, d):
+        at = pl.ds(h * (nel // 2), nel // 2)
+        return remote(w_ref.at[:, pl.ds(ch * nel + h * (nel // 2), nel // 2)],
+                      arr[ch].at[pl.ds(me * per, per), at],
+                      xsem.at[0, ch, d, h], xsem.at[1, ch, d, h], (to, col))
+
+    def wx_in(ch, d, h):
         origin = ((chip - d + chips) % chips) * 2 + core
-        return arr[ch].at[pl.ds(origin * per, per)]
+        return arr[ch].at[pl.ds(origin * per, per), pl.ds(h * (nel // 2), nel // 2)]
 
     def ws(ch):
         return remote(w_ref.at[:, chunk(ch)], arr[ch].at[pl.ds(me * per, per)],
                       wsem.at[0, ch, 0], wsem.at[1, ch, 0], (sib, col))
 
-    def wf(ch, d):
-        block = wx_in(ch, d)
-        return remote(block, block, wsem.at[2, ch, d], wsem.at[3, ch, d], (sib, col))
+    def wf(ch, d, h):
+        block = wx_in(ch, d, h)
+        return remote(block, block, xsem.at[2, ch, d, h], xsem.at[3, ch, d, h], (sib, col))
 
     def own(ch):
         return pltpu.make_async_copy(
@@ -89,25 +91,32 @@
     def landed(ref, sem):
         remote(ref, ref, sem, sem, (sib, col)).wait_recv()
 
+    def send_chunk(ch, d):
+        for h in range(2):
+            go(wx(ch, d, h))
+
     def walkers_in(ch):
         for d in range(1, chips):
-            landed(wx_in(ch, d), wsem.at[1, ch, d])
-            go(wf(ch, d))
+            for h in range(2):
+                landed(wx_in(ch, d, h), xsem.at[1, ch, d, h])
+                go(wf(ch, d, h))
         if ch + 2 < nch:
             for d in range(1, chips):
-                go(wx(ch + 2, d))
+                send_chunk(ch + 2, d)
 
     def walkers_all(ch):
         own(ch).wait()
         landed(arr[ch].at[pl.ds(sib * per, per)], wsem.at[1, ch, 0])
         for d in range(1, chips):
             origin = ((chip - d + chips) % chips) * 2 + (1 - core)
-            landed(arr[ch].at[pl.ds(origin * per, per)], wsem.at[3, ch, d])
+            for h in range(2):
+                landed(arr[ch].at[pl.ds(origin * per, per), pl.ds(h * (nel // 2), nel // 2)],
+                       xsem.at[3, ch, d, h])
 
     for k in range(1, nw):
         go(remote(cbuf, call.at[me], csend.at[k], crecv.at[k], ((me + k) % nw, col)))
     for d in range(1, chips):
-        go(wx(0, d))
+        send_chunk(0, d)
     for ch in range(nch):
         own(ch).start()
         go(ws(ch))
@@ -156,7 +165,7 @@
 
     pump(1)
     for d in range(1, chips):
-        go(wx(1, d))
+        send_chunk(1, d)
     pump(1)
     walkers_in(0)
 
@@ -295,7 +304,8 @@
             dma((nw,)),
             dma((nw,)),
             dma((1,)),
-            dma((4, nch, nw // 2)),
+            dma((3, nch, 1)),
+            dma((4, nch, nw // 2, 2)),
             dma((2, 2, half, 2)),
             dma((2, 2, half, 2)),
         ],

time: 46.7 us -> 47.1 us (level)
  no operation moved by 1% of the time
where the time goes in v3:
time: 47.1 us; the launch traced here: 47 us
  Pallas kernels  42.6 us (90%)
  local copies, waits for them, and re-layouts  3.73 us (8%)
  between operations  0.65 us (1%)
    pallas_call x1, Pallas kernels, body(): pl.pallas_call(functools.partial(kernel, nw, nc), out_shape=(jax.ShapeDty...  42.6 us
    unnamed x4, local copies, waits for them, and re-layouts  3.73 us

profile of v3, /device:TPU:0, one launch (start us, length us, event | category | flops | bytes accessed | tf_op | source)
XLA Modules:
  0.0 47.0 jit_solution(17762060440960798976)
XLA Ops:
  0.6 42.6 %shard_map.59 = (bf16[2,1024,256]{2,1,0:T(8,128)(2,1)}, f32[2,1024,256]{2,1,0:T(8,128)}) custom-call(s32[1,2]{1,0:T(1,128)} %bitcast.14, s32[1,2]{1,0:T(1,128)} %bitcast.15, bf16[256,1024]{1,0:T(8,128)(2,1)} %bitcast.13, bf16[2,1024,256]{2,1,0:T(8,128)(2,1)} %bitcast.11), custom_call_target="tpu_custom_call" | custom-call | tf_op jit(solution)/shard_map/pallas_call | solution.py:283
  43.2 0.0 copy-start
  43.2 2.4 %copy.10 = bf16[2,1,1024,256]{3,2,1,0:T(8,128)(2,1)} copy(bf16[2,1,1024,256]{3,2,1,0:T(8,128)(2,1)} %bitcast.12) | data formatting | bytes 2097152
  45.6 0.0 copy-done
  45.6 1.3 %copy.11 = f32[2,1,1024,256]{3,2,1,0:T(8,128)} copy(f32[2,1,1024,256]{3,2,1,0:T(8,128)S(1)} %bitcast.10) | data formatting | bytes 4194304
Async XLA Ops:
  43.2 2.4 %copy-start = (f32[2,1024,256]{2,1,0:T(8,128)S(1)}, f32[2,1024,256]{2,1,0:T(8,128)}, u32[]{:S(2)}) copy-start(f32[2,1024,256]{2,1,0:T(8,128)} %get-tuple-element.5) | copy-start | bytes 6291460
